TPU v7x, 32 devices: a whole 2x2x4 slice. The times are simulated.
32 devices in a mesh: slab: 2 (over x), gal: 4 (over y, core), qb: 4 (over z).
Axes of the slice: x: 2, y: 2, z: 4, core: 2. Of those that a mesh axis runs over, the one named last changes fastest.
Arguments:
- gallery: bfloat16 [16384, 768], P(('slab', 'gal')), parts along dimension 0, may hold values from -512 to 512
- querybank: bfloat16 [8, 2048, 768], P(('slab', 'qb'), 'gal'), parts along dimension 0, may hold values from -512 to 512
- test_queries: bfloat16 [8, 512, 768], P(('slab', 'qb'), 'gal'), parts along dimension 0, may hold values from -512 to 512
Outputs:
- logprob: float32 [4096, 8192], P(('slab', 'qb'), 'gal'), parts along dimension 0
- normalizer: float32 [16384], P(('slab', 'gal')), parts along dimension 0
There are 2 independent parts, one for each index of `slab`. A program takes and returns all parts, laid end to end along the dimension named above; each array names one. Nothing has to cross between parts.
All inputs are finite; a program needn't handle non-finite values.
Results may differ from a plain program's by a relative error of at most 0.00049.
Values may be sent and summed in bfloat16 or wider, within the bound.
A program may use at most 64 MiB of HBM per device.

v0:
```python
import math

import jax
import jax.numpy as jnp
from jax import lax
from jax.sharding import PartitionSpec as P

sharpness = 20.0


def unit_rows(values):
    wide = values.astype(jnp.float32)
    scaled = wide * lax.rsqrt(jnp.sum(wide * wide, axis=-1, keepdims=True) + 1e-06)
    return scaled.astype(jnp.bfloat16)


def column_terms(bank_block, gallery_unit):
    scores = lax.dot_general(
        bank_block, gallery_unit, (((1,), (1,)), ((), ())), preferred_element_type=jnp.float32
    )
    return jnp.sum(jnp.exp(sharpness * (scores - 1.0)), axis=0)


def bank_columns(bank_block, gallery_unit):
    rows = bank_block.shape[0]
    height = math.gcd(rows, 512)

    def add_block(index, running):
        piece = lax.dynamic_slice_in_dim(bank_block, index * height, height, 0)
        return running + column_terms(piece, gallery_unit)

    initial = jnp.zeros((gallery_unit.shape[0],), jnp.float32)
    return lax.fori_loop(0, rows // height, add_block, initial)


def per_device(gallery, querybank, test_queries):
    gallery_unit = unit_rows(gallery)
    bank_local = unit_rows(querybank[0])
    test_local = unit_rows(test_queries[0])
    bank_all = lax.all_gather(bank_local, "gal", axis=0, tiled=True)
    column_part = bank_columns(bank_all, gallery_unit)
    test_all = lax.all_gather(test_local, "gal", axis=0, tiled=True)
    column_total = lax.psum(column_part, "qb")
    normalizer = sharpness + jnp.log(column_total)
    bank_count = querybank.shape[1] * lax.axis_size("gal") * lax.axis_size("qb")
    offset = 2.0 * sharpness - math.log(bank_count)
    scores = lax.dot_general(
        test_all, gallery_unit, (((1,), (1,)), ((), ())), preferred_element_type=jnp.float32
    )
    logits = sharpness * scores - normalizer[None, :] - offset
    row_part = jnp.sum(jnp.exp(logits), axis=1)
    row_total = lax.psum(row_part, "gal")
    logprob = logits - jnp.log(row_total)[:, None]
    return (logprob, normalizer)


def solution(mesh):
    placed = (
        P(("slab", "gal"), None),
        P(("slab", "qb"), "gal", None),
        P(("slab", "qb"), "gal", None),
    )
    return jax.shard_map(
        per_device,
        mesh=mesh,
        in_specs=placed,
        out_specs=(P(("slab", "qb"), "gal"), P(("slab", "gal"))),
        check_vma=False,
    )
```

profile of v0, /device:TPU:0, one launch (start us, length us, event | category | flops | bytes accessed | tf_op | source)
XLA Modules:
  0.0 94.1 jit_solution(4073056862240279345)
XLA Ops:
  7.2 0.0 copy-start.1
  7.2 0.0 copy-start
  7.2 0.0 all-gather.2.cloned.1.call-start
  7.2 1.5 %fusion.5 = f32[512]{0:T(512)S(1)} fusion(bf16[1,512,768]{2,1,0:T(8,128)(2,1)} %param.6), kind=kLoop, calls=%fused_computation.13 | loop fusion | flops 1179136 | bytes 788480 | tf_op jit(solution)/shard_map/reduce_sum | solution.py:13
  8.8 2.2 %fusion.6 = bf16[512,768]{1,0:T(8,128)(2,1)} fusion(bf16[1,512,768]{2,1,0:T(8,128)(2,1)} %param.6, f32[512]{0:T(512)S(1)} %add_rsqrt_fusion.1), kind=kLoop, calls=%fused_computation.14 | loop fusion | flops 1179648 | bytes 1574912 | tf_op jit(solution)/shard_map/convert_element_type | solution.py:14
  11.0 0.0 all-gather.2.cloned.1.call-update
  11.0 1.0 %fusion.7 = f32[128]{0:T(128)S(1)} fusion(bf16[1,128,768]{2,1,0:T(8,128)(2,1)} %param.7), kind=kLoop, calls=%fused_computation.17 | loop fusion | flops 294784 | bytes 197120 | tf_op jit(solution)/shard_map/reduce_sum | solution.py:13
  12.1 0.0 copy-done
  12.1 0.7 fusion.2
  12.8 0.0 copy-done.1
  12.8 0.1 fusion.8
  12.9 10.6 %all_gather.6 = bf16[512,768]{1,0:T(8,128)(2,1)} all-gather(bf16[128,768]{1,0:T(8,128)(2,1)S(1)} %fusion.8), channel_id=1, replica_groups=mesh['slab'=2,'gal'=4,'qb'=4] {'gal'}, dimensions={0}, use_global_device_ids=true | all-gather | bytes 983040 | tf_op jit(solution)/shard_map/all_gather | solution.py:42
  23.4 2.3 %fusion.3 = bf16[2048,768]{1,0:T(8,128)(2,1)} fusion(bf16[2048,768]{1,0:T(8,128)(2,1)S(1)} %copy-done, f32[2048]{0:T(1024)S(1)} %add_rsqrt_fusion), kind=kLoop, calls=%fused_computation.7 | loop fusion | flops 4718592 | bytes 6299648 | tf_op jit(solution)/shard_map/convert_element_type | solution.py:14
  25.7 16.7 %all-gather.2.cloned.1.call-done = bf16[2048,768]{1,0:T(8,128)(2,1)} async-done(((bf16[512,768]{1,0:T(8,128)(2,1)}), bf16[2048,768]{1,0:T(8,128)(2,1)}) %all-gather.2.cloned.1.call-update) | async-done | bytes 3145744 | tf_op jit(solution)/shard_map/all_gather | solution.py:40
  42.4 0.0 copy-start.2
  42.4 16.3 %while.16 = (s32[]{:T(128)}, f32[2048]{0:T(1024)S(1)}, bf16[2048,768]{1,0:T(8,128)(2,1)}, bf16[2048,768]{1,0:T(8,128)(2,1)}, s32[]{:T(128)}, /*index=5*/s32[]{:T(128)}, s32[]{:T(128)}, s32[]{:T(128)}) while((s32[]{:T(128)}, f32[2048]{0:T(1024)S(1)}, bf16[2048,768]{1,0:T(8,128)(2,1)}, bf16[2048,768]{1,0:T(8,128)(2,1)}, s32[]{:T(128)}, ...), condition=%wide.region_5.0_spmd.clone, body=%wide.region_3.0_spmd.clone.sunk | while | flops 1613760512 | bytes 3965081 | solution.py:33
  42.4 4.1 %exponential_reduce_fusion.3 = f32[2048]{0:T(1024)S(1)} fusion(bf16[2048,768]{1,0:T(8,128)(2,1)} %get-tuple-element.182, bf16[2048,768]{1,0:T(8,128)(2,1)} %get-tuple-element.181, s32[]{:T(128)S(6)} %select_n.12), kind=kOutput, calls=%fused_computation.clone.1 | convolution fusion | flops 1613756416 | bytes 3940356 | tf_op jit(solution)/shard_map/while/body/eval_jaxpr/dot_general | solution.py:18
  46.5 4.0 %exponential_reduce_fusion.3 = f32[2048]{0:T(1024)S(1)} fusion(bf16[2048,768]{1,0:T(8,128)(2,1)} %get-tuple-element.182, bf16[2048,768]{1,0:T(8,128)(2,1)} %get-tuple-element.181, s32[]{:T(128)S(6)} %select_n.12), kind=kOutput, calls=%fused_computation.clone.1 | convolution fusion | flops 1613756416 | bytes 3940356 | tf_op jit(solution)/shard_map/while/body/eval_jaxpr/dot_general | solution.py:18
  50.6 4.0 %exponential_reduce_fusion.3 = f32[2048]{0:T(1024)S(1)} fusion(bf16[2048,768]{1,0:T(8,128)(2,1)} %get-tuple-element.182, bf16[2048,768]{1,0:T(8,128)(2,1)} %get-tuple-element.181, s32[]{:T(128)S(6)} %select_n.12), kind=kOutput, calls=%fused_computation.clone.1 | convolution fusion | flops 1613756416 | bytes 3940356 | tf_op jit(solution)/shard_map/while/body/eval_jaxpr/dot_general | solution.py:18
  54.6 4.0 %exponential_reduce_fusion.3 = f32[2048]{0:T(1024)S(1)} fusion(bf16[2048,768]{1,0:T(8,128)(2,1)} %get-tuple-element.182, bf16[2048,768]{1,0:T(8,128)(2,1)} %get-tuple-element.181, s32[]{:T(128)S(6)} %select_n.12), kind=kOutput, calls=%fused_computation.clone.1 | convolution fusion | flops 1613756416 | bytes 3940356 | tf_op jit(solution)/shard_map/while/body/eval_jaxpr/dot_general | solution.py:18
  58.7 11.8 %psum.14 = f32[2048]{0:T(1024)S(1)} all-reduce(f32[2048]{0:T(1024)S(1)} %get-tuple-element.112), channel_id=1, replica_groups=mesh['slab'=2,'gal'=4,'qb'=4] {'qb'}, use_global_device_ids=true, to_apply=%region_6.0 | all-reduce | flops 2048 | bytes 16384 | tf_op jit(solution)/shard_map/psum | solution.py:43
  70.5 0.0 copy-done.2
  70.5 0.0 copy-start.3
  70.6 6.0 %exponential_reduce_fusion.1 = (f32[512]{0:T(512)S(1)}, f32[512,2048]{1,0:T(8,128)}) fusion(f32[2048]{0:T(1024)S(1)} %log_add_fusion, bf16[512,768]{1,0:T(8,128)(2,1)S(1)} %copy-done.2, bf16[2048,768]{1,0:T(8,128)(2,1)} %get-tuple-element.188), kind=kOutput, calls=%fused_computation.8 | convolution fusion | flops 1614806528 | bytes 8136704 | tf_op jit(solution)/shard_map/dot_general | solution.py:47
  76.5 5.9 %psum.15 = f32[512]{0:T(512)S(1)} all-reduce(f32[512]{0:T(512)S(1)} %get-tuple-element.136), channel_id=1, replica_groups=mesh['slab'=2,'gal'=4,'qb'=4] {'gal'}, use_global_device_ids=true, to_apply=%region_8.0 | all-reduce | flops 512 | bytes 4096 | tf_op jit(solution)/shard_map/psum | solution.py:52
  82.4 0.0 copy-done.3
  82.4 4.8 %fusion.4 = f32[512,2048]{1,0:T(8,128)} fusion(f32[512,2048]{1,0:T(8,128)} %get-tuple-element.137, f32[512]{0:T(512)S(1)} %log.7, f32[2048]{0:T(1024)S(1)} %log_add_fusion), kind=kLoop, calls=%fused_computation.10 | loop fusion | flops 4194304 | bytes 8398848 | tf_op jit(solution)/shard_map/sub | solution.py:53
  (10 shorter events, 0.1 us)
Async XLA Ops:
  7.2 5.6 %copy-start.1 = (bf16[1,128,768]{2,1,0:T(8,128)(2,1)S(1)}, bf16[1,128,768]{2,1,0:T(8,128)(2,1)}, u32[]{:S(2)}) copy-start(bf16[1,128,768]{2,1,0:T(8,128)(2,1)} %param.7) | copy-start | bytes 589828
  7.2 4.9 %copy-start = (bf16[2048,768]{1,0:T(8,128)(2,1)S(1)}, bf16[2048,768]{1,0:T(8,128)(2,1)}, u32[]{:S(2)}) copy-start(bf16[2048,768]{1,0:T(8,128)(2,1)} %param.5) | copy-start | bytes 9437188
  7.2 35.2 %all-gather.2.cloned.1.call-start = ((), (), s32[]{:S(2)}) async-start(), calls=%async_computation | async-start | bytes 3932160 | tf_op jit(solution)/shard_map/all_gather | solution.py:40
  42.4 28.2 %copy-start.2 = (bf16[512,768]{1,0:T(8,128)(2,1)S(1)}, bf16[512,768]{1,0:T(8,128)(2,1)}, u32[]{:S(2)}) copy-start(bf16[512,768]{1,0:T(8,128)(2,1)} %all_gather.6) | copy-start | bytes 2359300
  70.5 11.9 %copy-start.3 = (f32[2048]{0:T(1024)}, f32[2048]{0:T(1024)S(1)}, u32[]{:S(2)}) copy-start(f32[2048]{0:T(1024)S(1)} %log_add_fusion) | copy-start | bytes 24580
Sparse Core Ops, SparseCore 0:
  11.1 31.2 all-gather.1
where the time goes:
time: 94.4 us; the launch traced here: 94.1 us
  blocking collectives  28.3 us (30%)
  matrix products  22.1 us (23%)
  waiting for transfers between devices  16.7 us (18%)
  between operations  14.1 us (15%)
  other arithmetic  12.7 us (13%)
    all_gather x1, waiting for transfers between devices, per_device(): bank_all = lax.all_gather(bank_local, 'gal', axis=0, tiled=True)  16.7 us
    dot_general x4, matrix products, column_terms(): lax.dot_general(bank_block, gallery_unit, (((1,), (1,)), ((), ())), prefe...  16.1 us
    psum x1, blocking collectives, per_device(): column_total = lax.psum(column_part, 'qb')  11.8 us
    all_gather x1, blocking collectives, per_device(): test_all = lax.all_gather(test_local, 'gal', axis=0, tiled=True)  10.6 us
    dot_general x1, matrix products, per_device(): lax.dot_general(test_all, gallery_unit, (((1,), (1,)), ((), ())), preferr...  5.95 us
    psum x1, blocking collectives, per_device(): row_total = lax.psum(row_part, 'gal')  5.91 us
    sub x1, other arithmetic, per_device(): logprob = logits - jnp.log(row_total)[:, None]  4.79 us
    convert_element_type x3, other arithmetic, unit_rows(): return scaled.astype(jnp.bfloat16)  4.59 us
  transfers between devices with their start and end apart: 1, of which 1 were waited for; matrix products, arithmetic and copies ran while one was open for 4% of the time, Pallas kernels for 0%

commit v1 on v0

v1 whole, which is shorter than its diff:
```python
import functools
import math

import jax
import jax.numpy as jnp
from jax import lax
from jax.experimental import pallas as pl
from jax.experimental.pallas import tpu as pltpu
from jax.sharding import PartitionSpec as P

sharpness = 20.0
LOG2E = math.log2(math.e)
MESH = pl.DeviceIdType.MESH
WINDOW = 2


def unit(values):
    wide = values.astype(jnp.float32)
    total = jnp.sum(wide * wide, axis=-1, keepdims=True)
    return (wide * lax.rsqrt(total + 1e-06)).astype(jnp.bfloat16)


def score(rows, gallery):
    return lax.dot_general(
        rows, gallery, (((1,), (1,)), ((), ())), preferred_element_type=jnp.float32
    )


def kernel(
    gsize, qsize, gallery_hbm, bank_hbm, test_hbm,
    s_out, norm_out, row_out,
    gal, bank, test, s_buf, acc, weight, lanes, zbuf, rbuf,
    load_sem, store_sem, by_send, by_recv, bs_send, bs_recv,
    ty_send, ty_recv, ts_send, ts_recv, z_send, z_recv, r_send, r_recv,
):
    g = lax.axis_index("gal")
    q = lax.axis_index("qb")
    chips = gsize // 2
    y, core = g // 2, lax.rem(g, 2)
    sib = 2 * y + (1 - core)
    _, nb, _, cb, width = bank.shape
    _, nt, _, ct, _ = test.shape
    cols = gal.shape[0]
    bank_count = nb * cb * gsize * qsize

    loads = []
    for k in range(nb):
        loads.append(pltpu.make_async_copy(
            bank_hbm.at[pl.ds(k * cb, cb)], bank.at[y, k, core], load_sem.at[k]))
    for k in range(nt):
        loads.append(pltpu.make_async_copy(
            test_hbm.at[pl.ds(k * ct, ct)], test.at[y, k, core], load_sem.at[nb + k]))
    loads.append(pltpu.make_async_copy(gallery_hbm, gal, load_sem.at[nb + nt]))
    for copy in loads:
        copy.start()

    barrier = pltpu.get_barrier_semaphore()
    for d in range(1, gsize):
        pl.semaphore_signal(barrier, inc=1, device_id={"gal": lax.rem(g + d, gsize)}, device_id_type=MESH)
    for d in range(1, qsize):
        pl.semaphore_signal(barrier, inc=1, device_id={"qb": lax.rem(q + d, qsize)}, device_id_type=MESH)

    def across(array, sends, recvs, k, d):
        slot = array.at[y, k, core]
        there = lax.rem(y + d, chips)
        return pltpu.make_async_remote_copy(
            src_ref=slot, dst_ref=slot, send_sem=sends.at[k, d], recv_sem=recvs.at[k, d],
            device_id={"gal": 2 * there + core}, device_id_type=MESH)

    def arrival(array, sends, recvs, k, d):
        slot = array.at[lax.rem(y + chips - d, chips), k, core]
        return pltpu.make_async_remote_copy(
            src_ref=slot, dst_ref=slot, send_sem=sends.at[k, d], recv_sem=recvs.at[k, d],
            device_id={"gal": sib}, device_id_type=MESH)

    def beside(array, sends, recvs, k, d):
        slot = array.at[lax.rem(y + chips - d, chips), k, core]
        return pltpu.make_async_remote_copy(
            src_ref=slot, dst_ref=slot, send_sem=sends.at[k, d], recv_sem=recvs.at[k, d],
            device_id={"gal": sib}, device_id_type=MESH)

    def from_sib(array, sends, recvs, k, d):
        slot = array.at[lax.rem(y + chips - d, chips), k, 1 - core]
        return pltpu.make_async_remote_copy(
            src_ref=slot, dst_ref=slot, send_sem=sends.at[k, d], recv_sem=recvs.at[k, d],
            device_id={"gal": sib}, device_id_type=MESH)

    B = (bank, by_send, by_recv)
    BS = (bank, bs_send, bs_recv)
    T = (test, ty_send, ty_recv)
    TS = (test, ts_send, ts_recv)
    queue = [(B, BS, k) for k in range(nb)] + [(T, TS, k) for k in range(nt)]

    def push(i):
        if i < len(queue):
            far, near, k = queue[i]
            for d in range(1, chips):
                across(*far, k, d).start()

    for i, (far, near, k) in enumerate(queue):
        loads[i].wait()
        array = far[0]
        array[y, k, core] = unit(array[y, k, core])
        if i == 0:
            pl.semaphore_wait(barrier, gsize - 1 + qsize - 1)
        if i < WINDOW:
            push(i)
        beside(*near, k, 0).start()

    acc[...] = jnp.zeros_like(acc)
    loads[-1].wait()
    step_rows = math.gcd(cols, 64)

    @pl.loop(0, cols // step_rows)
    def _(i):
        at = pl.ds(pl.multiple_of(i * step_rows, step_rows), step_rows)
        gal[at, :] = unit(gal[at, :])

    block = math.gcd(cols, 512)

    def add_bank(slot, k):
        rows = bank[slot, k].reshape(2 * cb, width)
        for j in range(cols // block):
            at = slice(j * block, (j + 1) * block)
            part = score(rows, gal[at, :])
            part = jnp.exp2(part * (sharpness * LOG2E) - sharpness * LOG2E)
            acc[:, at] += jnp.sum(part.reshape(2 * cb // 8, 8, block), axis=0)

    stores = []

    def put_scores(slot, k):
        rows = test[slot, k].reshape(2 * ct, width)
        index = slot * nt + k
        for j in range(cols // block):
            at = slice(j * block, (j + 1) * block)
            part = score(rows, gal[at, :]) * sharpness
            s_buf[slot, 0, k, :, at] = part[:ct]
            s_buf[slot, 1, k, :, at] = part[ct:]
        for c in range(2):
            copy = pltpu.make_async_copy(
                s_buf.at[slot, c, k], s_out.at[slot, c, k], store_sem.at[slot, c, k])
            copy.start()
            stores.append(copy)

    def row_pass(slot, k):
        for c in range(2):
            total = jnp.zeros((ct, 128), jnp.float32)
            for j in range(cols // 128):
                at = slice(j * 128, (j + 1) * 128)
                part = s_buf[slot, c, k, :, at]
                total += jnp.exp2(part * LOG2E - sharpness * LOG2E) * weight[0:1, at]
            at = pl.multiple_of(((slot * 2 + c) * nt + k) * ct, ct)
            lanes[pl.ds(at, ct), :] = total

    for k in range(nb):
        from_sib(*BS, k, 0).wait_recv()
        add_bank(y, k)

    pending = None
    for i, (far, near, k) in enumerate(queue[:nb]):
        for d in range(1, chips):
            arrival(*far, k, d).wait_recv()
            beside(*near, k, d).start()
            across(*far, k, d).wait_send()
        push(i + WINDOW)
        if pending is not None:
            for d in range(1, chips):
                from_sib(*BS, pending, d).wait_recv()
                add_bank(lax.rem(y + chips - d, chips), pending)
        pending = k
    for d in range(1, chips):
        from_sib(*BS, pending, d).wait_recv()
        add_bank(lax.rem(y + chips - d, chips), pending)

    column = jnp.sum(acc[...], axis=0, keepdims=True)
    for j in range(cols // 128):
        zbuf[0, j:j + 1, :] = column[:, j * 128:(j + 1) * 128]

    def z_copy(d):
        return pltpu.make_async_remote_copy(
            src_ref=zbuf.at[0], dst_ref=zbuf.at[d], send_sem=z_send.at[d], recv_sem=z_recv.at[d],
            device_id={"qb": lax.rem(q + d, qsize)}, device_id_type=MESH)

    for d in range(1, qsize):
        z_copy(d).start()
    for k in range(nt):
        from_sib(*TS, k, 0).wait_recv()
        put_scores(y, k)
    for d in range(1, qsize):
        z_copy(d).wait_recv()
    total = zbuf[0]
    for d in range(1, qsize):
        total += zbuf[d]
    norm_out[...] = sharpness + jnp.log(total)
    scale = (bank_count * math.exp(-2.0 * sharpness)) / total
    for j in range(cols // 128):
        weight[0:1, j * 128:(j + 1) * 128] = scale[j:j + 1, :]
    for k in range(nt):
        row_pass(y, k)

    pending = None
    for i, (far, near, k) in enumerate(queue[nb:]):
        for d in range(1, chips):
            arrival(*far, k, d).wait_recv()
            beside(*near, k, d).start()
            across(*far, k, d).wait_send()
        push(nb + i + WINDOW)
        if pending is not None:
            for d in range(1, chips):
                slot = lax.rem(y + chips - d, chips)
                from_sib(*TS, pending, d).wait_recv()
                put_scores(slot, pending)
                row_pass(slot, pending)
        pending = k
    for d in range(1, chips):
        slot = lax.rem(y + chips - d, chips)
        from_sib(*TS, pending, d).wait_recv()
        put_scores(slot, pending)
        row_pass(slot, pending)

    rows = lanes.shape[0]
    rbuf[0] = jnp.zeros_like(rbuf[0])
    sums = jnp.sum(lanes[...].T, axis=0, keepdims=True)
    for j in range(rows // 128):
        rbuf[0, j:j + 1, :] = sums[:, j * 128:(j + 1) * 128]

    def r_copy(d):
        return pltpu.make_async_remote_copy(
            src_ref=rbuf.at[0], dst_ref=rbuf.at[d], send_sem=r_send.at[d], recv_sem=r_recv.at[d],
            device_id={"gal": lax.rem(g + d, gsize)}, device_id_type=MESH)

    for d in range(1, gsize):
        r_copy(d).start()
    for copy in stores:
        copy.wait()
    for i, (far, near, k) in enumerate(queue):
        for d in range(chips):
            beside(*near, k, d).wait_send()
    for d in range(1, qsize):
        z_copy(d).wait_send()
    for d in range(1, gsize):
        r_copy(d).wait()
    total = rbuf[0]
    for d in range(1, gsize):
        total += rbuf[d]
    row_out[...] = jnp.log(total)


def fused(gallery, bank, test, gsize, qsize):
    cols, width = gallery.shape
    rb, rt = bank.shape[0], test.shape[0]
    cb = math.gcd(rb, 128)
    ct = math.gcd(rt, 64)
    chips, nb, nt = gsize // 2, rb // cb, rt // ct
    rows = gsize * rt
    tall = -(-rows // 128 // 8) * 8
    dma = lambda *shape: pltpu.SemaphoreType.DMA(shape)
    f32 = jnp.float32
    scores, norm, row = pl.pallas_call(
        functools.partial(kernel, gsize, qsize),
        out_shape=(
            jax.ShapeDtypeStruct((chips, 2, nt, ct, cols), f32),
            jax.ShapeDtypeStruct((cols // 128, 128), f32),
            jax.ShapeDtypeStruct((tall, 128), f32),
        ),
        in_specs=[pl.BlockSpec(memory_space=pl.ANY)] * 3,
        out_specs=(
            pl.BlockSpec(memory_space=pl.ANY),
            pl.BlockSpec(memory_space=pltpu.VMEM),
            pl.BlockSpec(memory_space=pltpu.VMEM),
        ),
        scratch_shapes=[
            pltpu.VMEM((cols, width), jnp.bfloat16),
            pltpu.VMEM((chips, nb, 2, cb, width), jnp.bfloat16),
            pltpu.VMEM((chips, nt, 2, ct, width), jnp.bfloat16),
            pltpu.VMEM((chips, 2, nt, ct, cols), f32),
            pltpu.VMEM((8, cols), f32),
            pltpu.VMEM((8, cols), f32),
            pltpu.VMEM((rows, 128), f32),
            pltpu.VMEM((qsize, cols // 128, 128), f32),
            pltpu.VMEM((gsize, tall, 128), f32),
            dma(nb + nt + 1),
            dma(chips, 2, nt),
            dma(nb, chips), dma(nb, chips), dma(nb, chips), dma(nb, chips),
            dma(nt, chips), dma(nt, chips), dma(nt, chips), dma(nt, chips),
            dma(qsize), dma(qsize), dma(gsize), dma(gsize),
        ],
        compiler_params=pltpu.CompilerParams(
            collective_id=0, has_side_effects=True, vmem_limit_bytes=40 * 1024 * 1024
        ),
        cost_estimate=pl.CostEstimate(
            flops=2 * cols * width * gsize * (rb + rt),
            bytes_accessed=2 * width * (cols + rb + rt) + 4 * rows * cols,
            transcendentals=cols * gsize * (rb + rt),
        ),
    )(gallery, bank, test)
    return scores.reshape(rows, cols), norm.reshape(cols), row.reshape(-1)[:rows]


def per_device(gallery, querybank, test_queries):
    gsize, qsize = lax.axis_size("gal"), lax.axis_size("qb")
    bank_count = querybank.shape[1] * gsize * qsize
    offset = 2.0 * sharpness - math.log(bank_count)
    scores, normalizer, row_log = fused(gallery, querybank[0], test_queries[0], gsize, qsize)
    logprob = scores - (normalizer + offset)[None, :] - row_log[:, None]
    return (logprob, normalizer)


def solution(mesh):
    placed = (
        P(("slab", "gal"), None),
        P(("slab", "qb"), "gal", None),
        P(("slab", "qb"), "gal", None),
    )
    return jax.shard_map(
        per_device,
        mesh=mesh,
        in_specs=placed,
        out_specs=(P(("slab", "qb"), "gal"), P(("slab", "gal"))),
        check_vma=False,
    )
```

time: 94.4 us -> 46.2 us (0.49)
  Pallas kernels: 0 us -> 38.2 us
  blocking collectives: 28.3 us -> 0 us
  matrix products: 22.1 us -> 0 us
  waiting for transfers between devices: 16.7 us -> 0 us
  between operations: 14.1 us -> 0.66 us
  other arithmetic: 12.7 us -> 2.51 us
  local copies, waits for them, and re-layouts: 0.03 us -> 4.54 us
    pallas_call x0 -> x1, Pallas kernels: none -> 38.2 us  [fused(): pl.pallas_call(functools.partial(kernel, gsize, qsize), out_shape=(jax.Sh...]
    dot_general x5 -> x0, matrix products: 22.1 us -> none  [the longest x4 16.1 us: column_terms(): lax.dot_general(bank_block, gallery_unit, (((1,), (1,)), ((), ())), prefe...]
    psum x2 -> x0, blocking collectives: 17.8 us -> none  [the longest x1 11.8 us: per_device(): column_total = lax.psum(column_part, 'qb')]
    all_gather x1 -> x0, waiting for transfers between devices: 16.7 us -> none  [per_device(): bank_all = lax.all_gather(bank_local, 'gal', axis=0, tiled=True)]
    all_gather x1 -> x0, blocking collectives: 10.6 us -> none  [per_device(): test_all = lax.all_gather(test_local, 'gal', axis=0, tiled=True)]
    convert_element_type x3 -> x0, other arithmetic: 4.59 us -> none  [unit_rows(): return scaled.astype(jnp.bfloat16)]
    unnamed x8 -> x7, local copies, waits for them, and re-layouts: 0.02 us -> 4.54 us
    reduce_sum x3 -> x0, other arithmetic: 3.24 us -> none  [unit_rows(): jnp.sum(wide * wide, axis=-1, keepdims=True) + 1e-06]
  transfers between devices with their start and end apart: 1 -> 0, of which waited for: 1 -> 0; matrix products, arithmetic and copies ran while one was open for 4% -> 0% of each run, Pallas kernels for 0% -> 0%
where the time goes in v1:
time: 46.2 us; the launch traced here: 46 us
  Pallas kernels  38.2 us (83%)
  local copies, waits for them, and re-layouts  4.54 us (10%)
  other arithmetic  2.51 us (5%)
  between operations  0.66 us (1%)
    pallas_call x1, Pallas kernels, fused(): pl.pallas_call(functools.partial(kernel, gsize, qsize), out_shape=(jax.Sh...  38.2 us
    unnamed x7, local copies, waits for them, and re-layouts  4.54 us
    sub x1, other arithmetic, per_device(): logprob = scores - (normalizer + offset)[None, :] - row_log[:, None]  2.5 us

profile of v1, /device:TPU:0, one launch (start us, length us, event | category | flops | bytes accessed | tf_op | source)
XLA Modules:
  0.0 46.0 jit_solution(2615328014055430288)
XLA Ops:
  0.6 0.0 copy-start
  0.6 1.9 %copy-done = bf16[2048,768]{1,0:T(8,128)(2,1)S(1)} copy-done((bf16[2048,768]{1,0:T(8,128)(2,1)S(1)}, bf16[2048,768]{1,0:T(8,128)(2,1)}, u32[]{:S(2)}) %copy-start) | copy-done | bytes 3145752
  2.5 0.0 copy-start.1
  2.5 1.1 %copy-done.1 = bf16[1,512,768]{2,1,0:T(8,128)(2,1)S(1)} copy-done((bf16[1,512,768]{2,1,0:T(8,128)(2,1)S(1)}, bf16[1,512,768]{2,1,0:T(8,128)(2,1)}, u32[]{:S(2)}) %copy-start.1) | copy-done | bytes 786456
  3.7 0.0 copy-start.2
  3.7 0.9 %copy-done.2 = bf16[1,128,768]{2,1,0:T(8,128)(2,1)S(1)} copy-done((bf16[1,128,768]{2,1,0:T(8,128)(2,1)S(1)}, bf16[1,128,768]{2,1,0:T(8,128)(2,1)}, u32[]{:S(2)}) %copy-start.2) | copy-done | bytes 196632
  4.6 38.2 %shard_map.50 = (f32[2,2,2,64,2048]{4,3,2,1,0:T(8,128)S(1)}, f32[16,128]{1,0:T(8,128)S(1)}, f32[8,128]{1,0:T(8,128)S(1)}) custom-call(bf16[2048,768]{1,0:T(8,128)(2,1)S(1)} %copy-done, bf16[512,768]{1,0:T(8,128)(2,1)S(1)} %bitcast.11, bf16[128,768]{1,0:T(8,128)(2,1)S(1)} %bitcast.12), custom_call_target="tpu_custom_call" | custom-call | flops 8053063680 | bytes 8323072 | tf_op jit(solution)/shard_map/pallas_call | solution.py:259
  42.9 2.5 %fusion = f32[512,2048]{1,0:T(8,128)} fusion(f32[2,2,2,64,2048]{4,3,2,1,0:T(8,128)S(1)} %get-tuple-element.5, f32[512]{0:T(512)S(1)} %slice_bitcast_fusion, f32[2048]{0:T(1024)S(1)} %broadcast_add_fusion), kind=kLoop, calls=%fused_computation.1 | loop fusion | flops 2097152 | bytes 8398848 | tf_op jit(solution)/shard_map/sub | solution.py:305
  45.4 0.6 %copy.6 = f32[2048]{0:T(1024)} copy(f32[2048]{0:T(1024)S(1)} %bitcast.10) | data formatting | bytes 16384
  (2 shorter events, 0.0 us)
Async XLA Ops:
  0.6 1.9 %copy-start = (bf16[2048,768]{1,0:T(8,128)(2,1)S(1)}, bf16[2048,768]{1,0:T(8,128)(2,1)}, u32[]{:S(2)}) copy-start(bf16[2048,768]{1,0:T(8,128)(2,1)} %gallery_hbm.1) | copy-start | bytes 9437188
  2.5 1.1 %copy-start.1 = (bf16[1,512,768]{2,1,0:T(8,128)(2,1)S(1)}, bf16[1,512,768]{2,1,0:T(8,128)(2,1)}, u32[]{:S(2)}) copy-start(bf16[1,512,768]{2,1,0:T(8,128)(2,1)} %param.4) | copy-start | bytes 2359300
  3.7 0.9 %copy-start.2 = (bf16[1,128,768]{2,1,0:T(8,128)(2,1)S(1)}, bf16[1,128,768]{2,1,0:T(8,128)(2,1)}, u32[]{:S(2)}) copy-start(bf16[1,128,768]{2,1,0:T(8,128)(2,1)} %param.5) | copy-start | bytes 589828

commit v2 on v1

--- a/solution.py
+++ b/solution.py
@@ -28,9 +28,9 @@
 
 def kernel(
     gsize, qsize, gallery_hbm, bank_hbm, test_hbm,
-    s_out, norm_out, row_out,
-    gal, bank, test, s_buf, acc, weight, lanes, zbuf, rbuf,
-    load_sem, store_sem, by_send, by_recv, bs_send, bs_recv,
+    s_buf, norm_out, row_out,
+    gal, bank, test, acc, weight, lanes, zbuf, rbuf,
+    load_sem, by_send, by_recv, bs_send, bs_recv,
     ty_send, ty_recv, ts_send, ts_recv, z_send, z_recv, r_send, r_recv,
 ):
     g = lax.axis_index("gal")
@@ -126,21 +126,13 @@
             part = jnp.exp2(part * (sharpness * LOG2E) - sharpness * LOG2E)
             acc[:, at] += jnp.sum(part.reshape(2 * cb // 8, 8, block), axis=0)
 
-    stores = []
-
     def put_scores(slot, k):
         rows = test[slot, k].reshape(2 * ct, width)
-        index = slot * nt + k
         for j in range(cols // block):
             at = slice(j * block, (j + 1) * block)
             part = score(rows, gal[at, :]) * sharpness
             s_buf[slot, 0, k, :, at] = part[:ct]
             s_buf[slot, 1, k, :, at] = part[ct:]
-        for c in range(2):
-            copy = pltpu.make_async_copy(
-                s_buf.at[slot, c, k], s_out.at[slot, c, k], store_sem.at[slot, c, k])
-            copy.start()
-            stores.append(copy)
 
     def row_pass(slot, k):
         for c in range(2):
@@ -155,6 +147,9 @@
     for k in range(nb):
         from_sib(*BS, k, 0).wait_recv()
         add_bank(y, k)
+    for k in range(nt):
+        from_sib(*TS, k, 0).wait_recv()
+        put_scores(y, k)
 
     pending = None
     for i, (far, near, k) in enumerate(queue[:nb]):
@@ -183,9 +178,6 @@
 
     for d in range(1, qsize):
         z_copy(d).start()
-    for k in range(nt):
-        from_sib(*TS, k, 0).wait_recv()
-        put_scores(y, k)
     for d in range(1, qsize):
         z_copy(d).wait_recv()
     total = zbuf[0]
@@ -231,8 +223,6 @@
 
     for d in range(1, gsize):
         r_copy(d).start()
-    for copy in stores:
-        copy.wait()
     for i, (far, near, k) in enumerate(queue):
         for d in range(chips):
             beside(*near, k, d).wait_send()
@@ -263,9 +253,9 @@
             jax.ShapeDtypeStruct((cols // 128, 128), f32),
             jax.ShapeDtypeStruct((tall, 128), f32),
         ),
-        in_specs=[pl.BlockSpec(memory_space=pl.ANY)] * 3,
+        in_specs=[pl.BlockSpec(memory_space=pltpu.HBM)] * 3,
         out_specs=(
-            pl.BlockSpec(memory_space=pl.ANY),
+            pl.BlockSpec(memory_space=pltpu.VMEM),
             pl.BlockSpec(memory_space=pltpu.VMEM),
             pl.BlockSpec(memory_space=pltpu.VMEM),
         ),
@@ -273,14 +263,12 @@
             pltpu.VMEM((cols, width), jnp.bfloat16),
             pltpu.VMEM((chips, nb, 2, cb, width), jnp.bfloat16),
             pltpu.VMEM((chips, nt, 2, ct, width), jnp.bfloat16),
-            pltpu.VMEM((chips, 2, nt, ct, cols), f32),
             pltpu.VMEM((8, cols), f32),
             pltpu.VMEM((8, cols), f32),
             pltpu.VMEM((rows, 128), f32),
             pltpu.VMEM((qsize, cols // 128, 128), f32),
             pltpu.VMEM((gsize, tall, 128), f32),
             dma(nb + nt + 1),
-            dma(chips, 2, nt),
             dma(nb, chips), dma(nb, chips), dma(nb, chips), dma(nb, chips),
             dma(nt, chips), dma(nt, chips), dma(nt, chips), dma(nt, chips),
             dma(qsize), dma(qsize), dma(gsize), dma(gsize),
@@ -293,7 +281,7 @@
             bytes_accessed=2 * width * (cols + rb + rt) + 4 * rows * cols,
             transcendentals=cols * gsize * (rb + rt),
         ),
-    )(gallery, bank, test)
+    )(*(pltpu.with_memory_space_constraint(x, pltpu.HBM) for x in (gallery, bank, test)))
     return scores.reshape(rows, cols), norm.reshape(cols), row.reshape(-1)[:rows]
 
 

time: 46.2 us -> 42.7 us (0.924)
  local copies, waits for them, and re-layouts: 4.54 us -> 0.6 us
  Pallas kernels: 38.2 us -> 38.7 us
    unnamed x7 -> x1, local copies, waits for them, and re-layouts: 4.54 us -> 0.6 us
    pallas_call x1, Pallas kernels: 38.2 us -> 38.7 us  [fused(): pl.pallas_call(functools.partial(kernel, gsize, qsize), out_shape=(jax.Sh...]
where the time goes in v2:
time: 42.7 us; the launch traced here: 42.5 us
  Pallas kernels  38.7 us (91%)
  other arithmetic  2.51 us (6%)
  between operations  0.65 us (2%)
  local copies, waits for them, and re-layouts  0.6 us (1%)
    pallas_call x1, Pallas kernels, fused(): pl.pallas_call(functools.partial(kernel, gsize, qsize), out_shape=(jax.Sh...  38.7 us
    sub x1, other arithmetic, per_device(): logprob = scores - (normalizer + offset)[None, :] - row_log[:, None]  2.5 us

profile of v2, /device:TPU:0, one launch (start us, length us, event | category | flops | bytes accessed | tf_op | source)
XLA Modules:
  0.0 42.5 jit_solution(15162270311894535817)
XLA Ops:
  0.6 38.7 %shard_map.50 = (f32[2,2,2,64,2048]{4,3,2,1,0:T(8,128)S(1)}, f32[16,128]{1,0:T(8,128)S(1)}, f32[8,128]{1,0:T(8,128)S(1)}) custom-call(bf16[2048,768]{1,0:T(8,128)(2,1)} %gallery_hbm.1, bf16[512,768]{1,0:T(8,128)(2,1)} %bitcast.11, bf16[128,768]{1,0:T(8,128)(2,1)} %bitcast.12), custom_call_target="tpu_custom_call" | custom-call | flops 8053063680 | bytes 8323072 | tf_op jit(solution)/shard_map/pallas_call | solution.py:249
  39.4 2.5 %fusion = f32[512,2048]{1,0:T(8,128)} fusion(f32[2,2,2,64,2048]{4,3,2,1,0:T(8,128)S(1)} %get-tuple-element.5, f32[512]{0:T(512)S(1)} %slice_bitcast_fusion, f32[2048]{0:T(1024)S(1)} %broadcast_add_fusion), kind=kLoop, calls=%fused_computation.1 | loop fusion | flops 2097152 | bytes 8398848 | tf_op jit(solution)/shard_map/sub | solution.py:293
  41.9 0.6 %copy.6 = f32[2048]{0:T(1024)} copy(f32[2048]{0:T(1024)S(1)} %bitcast.10) | data formatting | bytes 16384
  (2 shorter events, 0.0 us)

commit v3 on v2

--- a/solution.py
+++ b/solution.py
@@ -11,7 +11,7 @@
 sharpness = 20.0
 LOG2E = math.log2(math.e)
 MESH = pl.DeviceIdType.MESH
-WINDOW = 2
+WINDOW = 3
 
 
 def unit(values):
@@ -178,18 +178,6 @@
 
     for d in range(1, qsize):
         z_copy(d).start()
-    for d in range(1, qsize):
-        z_copy(d).wait_recv()
-    total = zbuf[0]
-    for d in range(1, qsize):
-        total += zbuf[d]
-    norm_out[...] = sharpness + jnp.log(total)
-    scale = (bank_count * math.exp(-2.0 * sharpness)) / total
-    for j in range(cols // 128):
-        weight[0:1, j * 128:(j + 1) * 128] = scale[j:j + 1, :]
-    for k in range(nt):
-        row_pass(y, k)
-
     pending = None
     for i, (far, near, k) in enumerate(queue[nb:]):
         for d in range(1, chips):
@@ -202,13 +190,24 @@
                 slot = lax.rem(y + chips - d, chips)
                 from_sib(*TS, pending, d).wait_recv()
                 put_scores(slot, pending)
-                row_pass(slot, pending)
         pending = k
     for d in range(1, chips):
         slot = lax.rem(y + chips - d, chips)
         from_sib(*TS, pending, d).wait_recv()
         put_scores(slot, pending)
-        row_pass(slot, pending)
+
+    for d in range(1, qsize):
+        z_copy(d).wait_recv()
+    total = zbuf[0]
+    for d in range(1, qsize):
+        total += zbuf[d]
+    norm_out[...] = sharpness + jnp.log(total)
+    scale = (bank_count * math.exp(-2.0 * sharpness)) / total
+    for j in range(cols // 128):
+        weight[0:1, j * 128:(j + 1) * 128] = scale[j:j + 1, :]
+    for slot in range(chips):
+        for k in range(nt):
+            row_pass(slot, k)
 
     rows = lanes.shape[0]
     rbuf[0] = jnp.zeros_like(rbuf[0])

time: 42.7 us -> 38.1 us (0.89)
  Pallas kernels: 38.7 us -> 34.1 us
    pallas_call x1, Pallas kernels: 38.7 us -> 34.1 us  [fused(): pl.pallas_call(functools.partial(kernel, gsize, qsize), out_shape=(jax.Sh...]
where the time goes in v3:
time: 38.1 us; the launch traced here: 37.9 us
  Pallas kernels  34.1 us (90%)
  other arithmetic  2.51 us (7%)
  between operations  0.65 us (2%)
  local copies, waits for them, and re-layouts  0.6 us (2%)
    pallas_call x1, Pallas kernels, fused(): pl.pallas_call(functools.partial(kernel, gsize, qsize), out_shape=(jax.Sh...  34.1 us
    sub x1, other arithmetic, per_device(): logprob = scores - (normalizer + offset)[None, :] - row_log[:, None]  2.5 us

profile of v3, /device:TPU:0, one launch (start us, length us, event | category | flops | bytes accessed | tf_op | source)
XLA Modules:
  0.0 37.9 jit_solution(8547134906606082772)
XLA Ops:
  0.6 34.1 %shard_map.50 = (f32[2,2,2,64,2048]{4,3,2,1,0:T(8,128)S(1)}, f32[16,128]{1,0:T(8,128)S(1)}, f32[8,128]{1,0:T(8,128)S(1)}) custom-call(bf16[2048,768]{1,0:T(8,128)(2,1)} %gallery_hbm.1, bf16[512,768]{1,0:T(8,128)(2,1)} %bitcast.11, bf16[128,768]{1,0:T(8,128)(2,1)} %bitcast.12), custom_call_target="tpu_custom_call" | custom-call | flops 8053063680 | bytes 8323072 | tf_op jit(solution)/shard_map/pallas_call | solution.py:248
  34.8 2.5 %fusion = f32[512,2048]{1,0:T(8,128)} fusion(f32[2,2,2,64,2048]{4,3,2,1,0:T(8,128)S(1)} %get-tuple-element.5, f32[512]{0:T(512)S(1)} %slice_bitcast_fusion, f32[2048]{0:T(1024)S(1)} %broadcast_add_fusion), kind=kLoop, calls=%fused_computation.1 | loop fusion | flops 2097152 | bytes 8398848 | tf_op jit(solution)/shard_map/sub | solution.py:292
  37.3 0.6 %copy.6 = f32[2048]{0:T(1024)} copy(f32[2048]{0:T(1024)S(1)} %bitcast.10) | data formatting | bytes 16384
  (2 shorter events, 0.0 us)

commit v4 on v3

--- a/solution.py
+++ b/solution.py
@@ -281,7 +281,28 @@
             transcendentals=cols * gsize * (rb + rt),
         ),
     )(*(pltpu.with_memory_space_constraint(x, pltpu.HBM) for x in (gallery, bank, test)))
-    return scores.reshape(rows, cols), norm.reshape(cols), row.reshape(-1)[:rows]
+    return scores.reshape(rows, cols), norm, row
+
+
+def finish(offset, s_ref, norm_ref, row_ref, out_hbm, norm_hbm, buf, sem, norm_sem):
+    rows, cols = s_ref.shape
+    norm_copy = pltpu.make_async_copy(norm_ref, norm_hbm, norm_sem)
+    norm_copy.start()
+    copies = []
+    for i in range(rows // 128):
+        at = slice(i * 128, (i + 1) * 128)
+        own = jnp.broadcast_to(row_ref[i:i + 1, :], (128, 128)).T + offset
+        for j in range(cols // 128):
+            to = slice(j * 128, (j + 1) * 128)
+            buf[at, to] = s_ref[at, to] - norm_ref[j:j + 1, :] - own
+        for h in range(2):
+            part = pl.ds(i * 128 + h * 64, 64)
+            copy = pltpu.make_async_copy(buf.at[part], out_hbm.at[part], sem.at[2 * i + h])
+            copy.start()
+            copies.append(copy)
+    for copy in copies:
+        copy.wait()
+    norm_copy.wait()
 
 
 def per_device(gallery, querybank, test_queries):
@@ -289,7 +310,23 @@
     bank_count = querybank.shape[1] * gsize * qsize
     offset = 2.0 * sharpness - math.log(bank_count)
     scores, normalizer, row_log = fused(gallery, querybank[0], test_queries[0], gsize, qsize)
-    logprob = scores - (normalizer + offset)[None, :] - row_log[:, None]
+    rows, cols = scores.shape
+    logprob, normalizer = pl.pallas_call(
+        functools.partial(finish, offset),
+        out_shape=(
+            jax.ShapeDtypeStruct((rows, cols), jnp.float32),
+            jax.ShapeDtypeStruct(normalizer.shape, jnp.float32),
+        ),
+        in_specs=[pl.BlockSpec(memory_space=pltpu.VMEM)] * 3,
+        out_specs=[pl.BlockSpec(memory_space=pltpu.HBM)] * 2,
+        scratch_shapes=[
+            pltpu.VMEM((rows, cols), jnp.float32),
+            pltpu.SemaphoreType.DMA((rows // 64,)),
+            pltpu.SemaphoreType.DMA(()),
+        ],
+        compiler_params=pltpu.CompilerParams(vmem_limit_bytes=16 * 1024 * 1024),
+    )(scores, normalizer, row_log)
+    normalizer = normalizer.reshape(-1)
     return (logprob, normalizer)
 
 

time: 38.1 us -> 37.3 us (0.979)
  other arithmetic: 2.51 us -> 0 us
  Pallas kernels: 34.1 us -> 36.5 us
  local copies, waits for them, and re-layouts: 0.6 us -> 0 us
    sub x1 -> x0, other arithmetic: 2.5 us -> none  [per_device(): logprob = scores - (normalizer + offset)[None, :] - row_log[:, None]]
    pallas_call x0 -> x1, Pallas kernels: none -> 2.37 us  [per_device(): pl.pallas_call(functools.partial(finish, offset), out_shape=(jax.ShapeDty...]
    unnamed x1 -> x0, local copies, waits for them, and re-layouts: 0.6 us -> none
where the time goes in v4:
time: 37.3 us; the launch traced here: 37.2 us
  Pallas kernels  36.5 us (98%)
  between operations  0.64 us (2%)
    pallas_call x1, Pallas kernels, fused(): pl.pallas_call(functools.partial(kernel, gsize, qsize), out_shape=(jax.Sh...  34.1 us
    pallas_call x1, Pallas kernels, per_device(): pl.pallas_call(functools.partial(finish, offset), out_shape=(jax.ShapeDty...  2.37 us

profile of v4, /device:TPU:0, one launch (start us, length us, event | category | flops | bytes accessed | tf_op | source)
XLA Modules:
  0.0 37.2 jit_solution(17370460066567226477)
XLA Ops:
  0.6 34.1 %shard_map.50 = (f32[2,2,2,64,2048]{4,3,2,1,0:T(8,128)S(1)}, f32[16,128]{1,0:T(8,128)S(1)}, f32[8,128]{1,0:T(8,128)S(1)}) custom-call(bf16[2048,768]{1,0:T(8,128)(2,1)} %gallery_hbm.1, bf16[512,768]{1,0:T(8,128)(2,1)} %bitcast.5, bf16[128,768]{1,0:T(8,128)(2,1)} %bitcast.6), custom_call_target="tpu_custom_call" | custom-call | flops 8053063680 | bytes 8323072 | tf_op jit(solution)/shard_map/pallas_call | solution.py:248
  34.8 2.4 %shard_map.51 = (f32[512,2048]{1,0:T(8,128)}, f32[16,128]{1,0:T(8,128)}) custom-call(f32[512,2048]{1,0:T(8,128)S(1)} %bitcast.4, f32[16,128]{1,0:T(8,128)S(1)} %get-tuple-element.8.norm_ref, f32[8,128]{1,0:T(8,128)S(1)} %get-tuple-element.9.row_ref), custom_call_target="tpu_custom_call" | custom-call | tf_op jit(solution)/shard_map/pallas_call | solution.py:314
